TPU v7x, 32 devices: a whole 2x2x4 slice. The times are simulated.
32 devices in a mesh: row: 8 (over z, y), col: 4 (over x, core).
Axes of the slice: x: 2, y: 2, z: 4, core: 2. Of those that a mesh axis runs over, the one named last changes fastest.
Arguments:
- tokens: bfloat16 [8192, 1024], P('row', 'col'), may hold values from -6 to 6
- segment_ids: int32 [8, 1024], P('row'), may hold values from 0 to 7, never falling along the last dimension, each value on 1 to 512 neighbouring positions
- w_query: bfloat16 [1024, 1024], P('row', 'col'), may hold values from -0.1875 to 0.1875
- key_matrix: bfloat16 [1024, 512], P('row', 'col'), may hold values from -0.1875 to 0.1875
- value_matrix: bfloat16 [1024, 512], P('row', 'col'), may hold values from -0.1875 to 0.1875
- w_out: bfloat16 [1024, 1024], P('col', 'row'), may hold values from -0.75 to 0.75
- w_gate: bfloat16 [1024, 4608], P('row', 'col'), may hold values from -0.1875 to 0.1875
- w_up: bfloat16 [1024, 4608], P('row', 'col'), may hold values from -0.1875 to 0.1875
- w_down: bfloat16 [4608, 1024], P('col', 'row'), may hold values from -0.09375 to 0.09375
- norm_attn: float32 [1024], replicated, may hold values from 0.1 to 1.9
- norm_ffn: float32 [1024], replicated, may hold values from 0.1 to 1.9
- norm_query: float32 [64], replicated, may hold values from 0.1 to 1.9
- norm_key: float32 [64], replicated, may hold values from 0.1 to 1.9
- cotangent: bfloat16 [8192, 1024], P('row', 'col'), may hold values from -6 to 6
Outputs:
- layer_out: bfloat16 [8192, 1024], P('row', 'col')
- grad_tokens: float32 [8192, 1024], P('row', 'col')
- grad_w_query: float32 [1024, 1024], P('row', 'col')
- grad_w_key: float32 [1024, 512], P('row', 'col')
- grad_w_value: float32 [1024, 512], P('row', 'col')
- grad_w_out: float32 [1024, 1024], P('col', 'row')
- grad_w_gate: float32 [1024, 4608], P('row', 'col')
- grad_w_up: float32 [1024, 4608], P('row', 'col')
- grad_w_down: float32 [4608, 1024], P('col', 'row')
- grad_norm_attn: float32 [1024], replicated
- grad_norm_ffn: float32 [1024], replicated
- grad_norm_query: float32 [64], replicated
- grad_norm_key: float32 [64], replicated
Inputs may be any that keep to these rules, and one draw needn't show every extreme that they name: `segment_ids`: within each sequence the ids never fall, and a document spans at most 512 tokens.
All inputs are finite; a program needn't handle non-finite values.
Results may differ from a plain program's by a relative error of at most 0.012.
The roundings to bfloat16 on the way count: a program that leaves them out, or rounds other values in their place, can miss the bound.
Values may be sent and summed in bfloat16 or wider, within the bound.
A program may use at most 192 MiB of HBM per device.

v0:
```python
import functools
import math

import jax
import jax.numpy as jnp
from jax import lax
from jax.experimental import pallas as pl
from jax.experimental.pallas import tpu as pltpu
from jax.sharding import PartitionSpec as P

epsilon = 1e-05
rope_base = 1000000.0
longest = 512
ids = 8
f32, bf16 = jnp.float32, jnp.bfloat16
MESH = pl.DeviceIdType.MESH
RB = 256


def dot_nn(a, b):
    return lax.dot_general(a, b, (((1,), (0,)), ((), ())), preferred_element_type=f32)


def dot_nt(a, b):
    return lax.dot_general(a, b, (((1,), (1,)), ((), ())), preferred_element_type=f32)


def rows(i, n):
    return pl.ds(pl.multiple_of(i * n, n), n)


AG_PAIRS, RS_PAIRS = (5, 6), (0, 1, 2)
ORDER = [
    ("owny", 0, "a"), ("ownz", 0, "a"), ("owny", 1, "a"), ("ownz", 1, "a"), ("gate_up", "a"), ("owny", 2, "a"),
    ("down", "a"), ("owny", 7, "a"), ("fwd", 0, 1, "e"), ("ownz", 2, "a"), ("toks", "a"), ("tables", "a"),
    ("cots", "a"), ("owny", 3, "a"), ("ownz", 7, "a"), ("fwd", 0, 1, "m"), ("fwd", 0, 2, "e"), ("fwd", 0, 2, "m"),
    ("fwd", 0, 3, "e"), ("fwd", 1, 1, "e"), ("fwd", 0, 3, "m"), ("tokf", "a"), ("fwd", 1, 1, "m"),
    ("fwd", 1, 2, "e"), ("fwd", 1, 2, "m"), ("owny", 5, "a"), ("fwd", 1, 3, "m"), ("ownz", 3, "a"), ("norm", "a"),
    ("fwd", 1, 3, "e"), ("fwd", 2, 1, "m"), ("fwd", 2, 2, "m"), ("owny", 4, "a"), ("owny", 6, "a"),
    ("ownz", 4, "a"), ("project", "a"), ("fwd", 2, 3, "m"), ("fwd", 3, 1, "m"), ("att", 0, "a"), ("aprod", 0, "a"),
    ("fwd", 4, 1, "e"), ("fwd", 2, 1, "e"), ("fwd", 3, 2, "m"), ("ownz", 5, "a"), ("amid", "a"), ("fwd", 5, 1, "m"),
    ("fwd", 3, 3, "m"), ("att", 1, "a"), ("fwd", 4, 1, "m"), ("cotf", "a"), ("fwd", 4, 2, "m"), ("fwd", 2, 2, "e"),
    ("aprod", 1, "a"), ("fwd", 4, 3, "m"), ("fwd", 3, 1, "e"), ("fwd", 5, 2, "m"), ("fwd", 7, 1, "m"),
    ("ownz", 6, "a"), ("aft", 0, "a"), ("fwd", 7, 1, "e"), ("fwd", 5, 3, "m"), ("fwd", 2, 3, "e"),
    ("fwd", 7, 2, "m"), ("fwd", 7, 3, "m"), ("fwd", 5, 1, "e"), ("aft", 1, "a"), ("fwd", 3, 2, "e"),
    ("fwd", 5, 2, "e"), ("fwd", 3, 3, "e"), ("fwd", 6, 1, "e"), ("nff", 0, "a"), ("fwd", 4, 2, "e"),
    ("nff", 1, "a"), ("fwd", 4, 3, "e"), ("ffn", 0, 0, "a"), ("fwd", 6, 2, "e"), ("fwd", 6, 1, "m"),
    ("fwd", 6, 2, "m"), ("fwd", 6, 3, "m"), ("ffn", 0, 1, "a"), ("wg", 0, "a"), ("ffn", 1, 0, "a"),
    ("ffn", 1, 1, "a"), ("fwd", 5, 3, "e"), ("wg", 1, "a"), ("fwd", 7, 2, "e"), ("fwd", 6, 3, "e"),
    ("gh", 0, 0, "a"), ("relay", 0, 0, "m"), ("gh", 0, 1, "a"), ("fwd", 7, 3, "e"), ("wg", 3, "a"),
    ("ffn", 2, 0, "a"), ("ffn", 2, 1, "a"), ("wg", 2, "a"), ("gh", 1, 0, "a"), ("gh", 2, 0, "a"), ("gnfp", 0, "a"),
    ("mid", 3, 0, "e"), ("gh", 1, 1, "a"), ("gnfm", "a"), ("relay", 0, 1, "m"), ("gh", 2, 1, "a"),
    ("mid", 3, 0, "m"), ("relay", 1, 0, "m"), ("gnfp", 1, "a"), ("wg", 5, "a"), ("mid", 3, 1, "e"), ("snd", 8, "a"),
    ("naft", 0, "a"), ("wg", 4, "a"), ("mid", 5, 0, "m"), ("relay", 2, 0, "m"), ("relay", 1, 1, "m"),
    ("naft", 1, "a"), ("mid", 5, 1, "m"), ("gmix", 0, "a"), ("mid", 3, 1, "m"), ("mid", 5, 0, "e"), ("ab", 0, "a"),
    ("mid", 5, 2, "m"), ("mid", 3, 2, "e"), ("mid", 5, 1, "e"), ("rlf", 0, "a"), ("rlf", 1, "a"),
    ("mid", 8, 0, "e"), ("mid", 8, 1, "e"), ("relay", 3, 0, "m"), ("relay", 2, 1, "m"), ("relay", 3, 1, "m"),
    ("mid", 5, 2, "e"), ("mid", 8, 0, "m"), ("mid", 3, 2, "m"), ("mid", 8, 2, "e"), ("gmix", 1, "a"), ("brp", "a"),
    ("mid", 4, 0, "e"), ("wg", 6, "a"), ("relay", 5, 0, "m"), ("brm", "a"), ("mid", 8, 1, "m"), ("mid", 4, 0, "m"),
    ("ab", 1, "a"), ("mid", 4, 1, "e"), ("pb", "a"), ("relay", 5, 1, "m"), ("mid", 8, 2, "m"), ("mid", 4, 1, "m"),
    ("gnp", "a"), ("mid", 6, 0, "e"), ("mid", 4, 2, "m"), ("relay", 8, 0, "m"), ("relay", 4, 0, "m"),
    ("wg", 7, "a"), ("mid", 6, 1, "e"), ("gnm", "a"), ("mid", 6, 0, "m"), ("relay", 8, 1, "m"), ("mid", 6, 2, "e"),
    ("brf", "a"), ("relay", 4, 1, "m"), ("mid", 6, 1, "m"), ("mid", 9, 0, "m"), ("mid", 7, 0, "e"),
    ("mid", 7, 0, "m"), ("mid", 6, 2, "m"), ("mid", 9, 0, "e"), ("vc", "a"), ("mid", 7, 1, "e"), ("pre", 2, "e"),
    ("pre", 1, "e"), ("relay", 6, 0, "m"), ("mid", 7, 1, "m"), ("mid", 9, 1, "m"), ("relay", 6, 1, "m"),
    ("fin", 5, "a"), ("pre", 2, "m"), ("mid", 9, 1, "e"), ("relay", 7, 0, "m"), ("pre", 1, "m"), ("mid", 9, 2, "m"),
    ("pre", 0, "e"), ("mid", 7, 2, "m"), ("mid", 4, 2, "e"), ("pre", 0, "m"), ("relay", 9, 0, "m"),
    ("relay", 9, 1, "m"), ("mid", 9, 2, "e"), ("fin", 8, "a"), ("relay", 7, 1, "m"), ("fin", 6, "a"), ("vy", "a"),
    ("fin", 4, "a"), ("mid", 7, 2, "e"), ("fin", 3, "a"), ("fin", 2, "a"), ("fin", 1, "a"), ("fin", 9, "a"),
    ("gnfin", "a"), ("fin", 7, "a"), ("fin", 0, "a"), ("lof", "a"), ("end", "a"),
]


def layer_kernel(
    plan,
    tok_h, seg_ref, wq_h, wk_h, wv_h, wo_h, wg_h, wu_h, wd_h, ga_ref, gf_ref, gq_ref, gk_ref, cot_h,
    lo_h, gt_h, gquery_h, gkey_h, gvalue_h, gout_h, ggate_h, gup_h, gdown_h, gain_ref,
    W, WO, WD, GFO, GFD, G, RY, RZ, RYP, RZP, GF, Tk, Ct, Nm, R1, PRE, QS, KS, VS, KT, VT, DO, MX, PB, A0, B0, S0,
    RES, NF, GG, HID, CS, SN, BIAS, INV, DQ, DKV, AC, BC, SC, LOC, VEC, VCOL, VSUM, VY, VZ,
    loc_sem, agz_s, agz_r, agy_s, agy_r, rsy_s, rsy_r, rsz_s, rsz_r,
    cag_s, cag_r, crs_s, crs_r, gn_s, gn_r, lo_s, lo_r, vec_s, vec_r, vz_s, vz_r, out_sem,
):
    nz, tree, CH, RCH, ag_pairs, rs_pairs, place = plan
    T, D = Tk.shape
    br = RY.shape[1]
    QW, KW = PRE.shape[1] // 2, PRE.shape[1] // 4
    PW = 2 * QW + 2 * KW
    F = HID.shape[1]
    FC = F // 3
    HB = RB // 2
    down0 = PW + 2 * F
    nb = T // RB
    CW = D // 4
    GQ = GG.at[:, pl.ds(PW, 2 * QW)]
    PN = GG.at[:, pl.ds(PW + 2 * QW, D)]
    row, col = lax.axis_index("row"), lax.axis_index("col")
    z, y = row // 2, row % 2
    x, c = col // 2, col % 2
    ypeer = (row + 1 - 2 * y, col)
    cpeer = (row, col + 1 - 2 * c)
    xpeer = (row, (1 - x) * 2 + c)
    dpeer = (row, (1 - x) * 2 + 1 - c)
    partner = z + 1 - 2 * (z % 2)
    is_middle = (z == 1) | (z == 2)
    near, far = 2 - z // 2, 3 - 3 * (z // 2)

    def zdev(zz):
        return (zz * 2 + y, col)

    def zsrc(k):
        return [z, partner, near, far][k] if tree else (z + nz - k) % nz

    def zto(i):
        return [near, far, partner, z][i]

    def rc(src, dst, ss, rs, dev):
        return pltpu.make_async_remote_copy(
            src_ref=src, dst_ref=dst, send_sem=ss, recv_sem=rs, device_id=dev, device_id_type=MESH
        )

    def loop(n, body, first=0):
        def step(i, carry):
            body(i)
            return carry

        lax.fori_loop(first, n, step, 0)

    own = rows(row, br)
    mine = pl.ds(pl.multiple_of(col * CW, CW), CW)
    local = [
        (wq_h, W.at[own, pl.ds(0, QW)]),
        (wk_h, W.at[own, pl.ds(QW, KW)]),
        (wv_h, W.at[own, pl.ds(QW + KW, KW)]),
        (wo_h, WO),
        (tok_h, Tk.at[:, mine]),
        (cot_h, Ct.at[:, mine]),
    ]
    for j in range(3):
        local.append((wg_h.at[:, pl.ds(FC * j, FC)], W.at[own, pl.ds(PW + 2 * FC * j, FC)]))
        local.append((wu_h.at[:, pl.ds(FC * j, FC)], W.at[own, pl.ds(PW + 2 * FC * j + FC, FC)]))
    local.append((wd_h, WD))
    local = [pltpu.make_async_copy(s, d, loc_sem.at[i]) for i, (s, d) in enumerate(local)]

    def wblk(ch, zz, yy):
        start, width = CH[ch]
        return W.at[rows(zz * 2 + yy, br), pl.ds(start, width)]

    def wpair(ch, zz):
        start, width = CH[ch]
        return W.at[rows(zz, 2 * br), pl.ds(start, width)]

    def ag_z(ch, k, src, slot, dev):
        b = wpair(ch, src) if ch in ag_pairs else wblk(ch, src, y)
        return rc(b, b, agz_s.at[ch, k], agz_r.at[ch, slot], zdev(dev))

    def ag_y(ch, k, src, yy):
        b = wblk(ch, src, yy)
        return rc(b, b, agy_s.at[ch, k], agy_r.at[ch, k], ypeer)

    def own_y(ch):
        ag_y(ch, 0, z, y).start()

    def own_z(ch):
        if ch in ag_pairs:
            ag_y(ch, 0, z, 1 - y).wait_recv()
        if tree:
            ag_z(ch, 0, z, 1, partner).start()
            ag_z(ch, 1, z, jnp.where(is_middle, 2, 3), near).start()
        else:
            loop(nz, lambda k: ag_z(ch, k, z, k, (z + k) % nz).start(), 1)

    def forward(ch, k, middle):
        if not tree:
            if k == 3 and middle:

                def step(k):
                    ag_z(ch, k, zsrc(k), k, z).wait_recv()
                    ag_y(ch, k, zsrc(k), y).start()

                loop(nz, step, 1)
            return
        relayed = middle and k >= 2
        if ch in ag_pairs and not relayed:
            return
        ag_z(ch, k, zsrc(k), k, partner).wait_recv()
        if relayed:
            ag_z(ch, k, zsrc(k), k, partner).start()
        if ch not in ag_pairs:
            ag_y(ch, k, zsrc(k), y).start()

    def ag_wait(ch):
        if not tree:
            loop(nz, lambda k: ag_y(ch, k, zsrc(k), 1 - y).wait_recv())
        elif ch in ag_pairs:
            ag_z(ch, 0, partner, 1, partner).wait_recv()

            @pl.when(jnp.logical_not(is_middle))
            def _():
                ag_z(ch, 0, near, 2, partner).wait_recv()
                ag_z(ch, 0, far, 3, partner).wait_recv()

        else:
            for k in range(4):
                ag_y(ch, k, zsrc(k), 1 - y).wait_recv()

    def ag_done(ch):
        if not tree:
            loop(nz, lambda k: ag_y(ch, k, zsrc(k), y).wait_send())
            loop(nz, lambda k: ag_z(ch, k, z, k, z).wait_send(), 1)
            return
        for k in range(1 if ch in ag_pairs else 4):
            ag_y(ch, k, zsrc(k), y).wait_send()
        ag_z(ch, 0, z, 1, partner).wait_send()
        ag_z(ch, 1, z, 2, near).wait_send()

        @pl.when(is_middle)
        def _():
            ag_z(ch, 2, near, 2, partner).wait_send()
            ag_z(ch, 3, far, 3, partner).wait_send()

    def cag(n, block, parts=1):
        def copy(i, d, dev, h):
            return rc(block(d, h), block(d, h), cag_s.at[n, h, i], cag_r.at[n, h, i], dev)

        def start(h=0):
            copy(0, col, cpeer, h).start()
            copy(1, col, xpeer, h).start()

        def forward(h=0):
            copy(1, (1 - x) * 2 + c, xpeer, h).wait_recv()
            copy(2, (1 - x) * 2 + c, cpeer, h).start()

        def wait(far):
            for h in range(parts):
                if far:
                    copy(2, (1 - x) * 2 + 1 - c, cpeer, h).wait_recv()
                else:
                    copy(0, x * 2 + 1 - c, cpeer, h).wait_recv()

        def done():
            for h in range(parts):
                copy(0, col, cpeer, h).wait_send()
                copy(1, col, xpeer, h).wait_send()
                copy(2, (1 - x) * 2 + c, cpeer, h).wait_send()

        return start, forward, wait, done

    def col_block(ref):
        return lambda d, h: ref.at[:, pl.ds(pl.multiple_of(d * CW, CW), CW)]

    def row_block(ref):
        return lambda d, h: ref.at[rows(d * 2 + h, HB), :]

    tok_start, tok_forward, tok_wait, tok_done = cag(0, col_block(Tk))
    cot_start, cot_forward, cot_wait, cot_done = cag(1, col_block(Ct))
    nf_start, nf_forward, nf_wait, nf_done = cag(2, row_block(NF), 2)
    rl_start, rl_forward, rl_wait, rl_done = cag(3, row_block(Ct), 2)

    def crs(n, A, B, S):
        def to_core(i, xx, cc):
            return rc(PB.at[rows(xx * 2 + cc, RB), :], A(xx), crs_s.at[n, i], crs_r.at[n, i], cpeer)

        def to_x(h):
            half = rows(h, HB)
            return rc(S.at[half, :], B.at[half, :], crs_s.at[n, 2 + h], crs_r.at[n, 2 + h], xpeer)

        def produce(half, part):
            def step(i):
                xx = jnp.where(i < 2, 1 - x, x)
                cc = jnp.where(i % 2 == 0, 1 - c, c)
                PB[rows(xx * 2 + cc, RB), :] = part(xx * 2 + cc).astype(bf16)

                @pl.when(i % 2 == 0)
                def _():
                    to_core(i // 2, xx, 1 - c).start()

            loop(2 * half + 2, step, 2 * half)

        def middle():
            to_core(0, 1 - x, c).wait_recv()

            def step(i):
                r = rows(i, 32)
                block = PB[pl.ds(pl.multiple_of(((1 - x) * 2 + c) * RB + i * 32, 32), 32), :]
                S[r, :] = (block.astype(f32) + A(1 - x)[r, :].astype(f32)).astype(bf16)

            for h in range(2):
                loop(HB // 32 * (h + 1), step, HB // 32 * h)
                to_x(h).start()

        def total(h, use):
            if h == 0:
                to_core(1, x, c).wait_recv()
            to_x(h).wait_recv()

            def step(i):
                r = rows(i, 32)
                at = pl.ds(pl.multiple_of(col * RB + i * 32, 32), 32)
                use(r, at, PB[at, :].astype(f32) + A(x)[r, :].astype(f32) + B[r, :].astype(f32))

            loop(HB // 32 * (h + 1), step, HB // 32 * h)

        def done():
            to_core(0, 1 - x, 1 - c).wait_send()
            to_core(1, x, 1 - c).wait_send()
            to_x(0).wait_send()
            to_x(1).wait_send()

        return produce, middle, total, done

    a_produce, a_middle, a_total, a_done = crs(0, lambda i: A0.at[i], B0, S0)
    n_produce, n_middle, n_total, n_done = crs(1, lambda i: A0.at[i], B0, S0)
    b_produce, b_middle, b_total, b_done = crs(
        2, lambda i: NF.at[rows(i, RB), :], NF.at[pl.ds(2 * RB, RB), :], NF.at[pl.ds(3 * RB, RB), :]
    )

    def other_first(half, i):
        return jnp.where(half == 0, 1 - x, x) * 2 + jnp.where(i == 0, 1 - c, c)

    def own_first(half, i):
        return jnp.where(half == 0, x, 1 - x) * 2 + jnp.where(i == 0, c, 1 - c)

    def rows_of_chip(mine_first, half, work):
        for xx in range(2):

            @pl.when(x == (xx if mine_first == (half == 0) else 1 - xx))
            def _():
                work(xx)

    def gcol(ch):
        start, width = RCH[ch]
        return (G, start - PW, width) if start >= PW else (GG, start, width)

    def gblk(ch, zz, yy):
        ref, start, width = gcol(ch)
        return ref.at[rows(zz * 2 + yy, br), pl.ds(start, width)]

    def part_of(ch):
        return pl.ds(place[ch], RCH[ch][1])

    def rs_y(ch, zz, yy):
        landing = RYP.at[:, part_of(ch)] if ch in rs_pairs else RY.at[zz, :, part_of(ch)]
        return rc(gblk(ch, zz, yy), landing, rsy_s.at[ch, zz], rsy_r.at[ch, zz], ypeer)

    def rs_z(ch, k, zz, slot, dev):
        if ch in rs_pairs:
            ref, start, width = gcol(ch)
            src, dst = ref.at[rows(zz, 2 * br), pl.ds(start, width)], RZP.at[slot, :, part_of(ch)]
        else:
            src, dst = RY.at[zz, :, part_of(ch)], RZ.at[slot, :, part_of(ch)]
        return rc(src, dst, rsz_s.at[ch, k], rsz_r.at[ch, slot], zdev(dev))

    zper = RB // (2 * br)

    def weight_grad(left, pieces):
        def one(i, d):
            lt = jnp.transpose(left[:, rows(d, RB)])
            for ch, right in pieces:
                ref, start, width = gcol(ch)
                ref[rows(d, RB), pl.ds(start, right.shape[1])] = dot_nn(lt, right[...]).astype(bf16)
                if ch not in rs_pairs:
                    loop(zper, lambda s: rs_y(ch, d * zper + s, 1 - y).start())
                else:

                    @pl.when((i == 2) | ((i < 2) & jnp.logical_not(is_middle)))
                    def _():
                        rs_z(ch, i, d, i, partner).start()

        if tree:

            def step(i):
                one(i, jnp.where(i == 0, near, jnp.where(i == 1, far, jnp.where(i == 2, partner, z))))

            loop(4, step)
        else:
            loop(D // RB, lambda i: one(i, (row * br // RB + 1 + i) % (D // RB)))

    def send_grad(ch):
        if tree:
            for i in range(4):
                rs_y(ch, zto(i), 1 - y).start()
        else:
            loop(nz, lambda k: rs_y(ch, k, 1 - y).start())

    def rs_mid(ch, i, middle):
        ref, gstart, width = gcol(ch)

        def one(zz):
            rs_y(ch, zz, y).wait_recv()

            def add(j):
                r = rows(j, 16)
                g = ref[pl.ds(pl.multiple_of((zz * 2 + y) * br + j * 16, 16), 16), pl.ds(gstart, width)]
                t = RY[zz, r, part_of(ch)]
                RY[zz, r, part_of(ch)] = (g.astype(f32) + t.astype(f32)).astype(bf16)

            loop(br // 16, add)

        if not tree:
            if i == 2 and middle:

                def step(k):
                    zz = (z + k) % nz
                    one(zz)
                    rs_z(ch, k, zz, k - 1, zz).start()

                loop(nz, step, 1)
        elif ch not in rs_pairs:
            one(zto(i))
            if i == 2 or not middle:
                rs_z(ch, i, zto(i), i, partner).start()

    def rs_relay(ch, i):
        if not tree:
            return
        zz = zto(i)
        rs_z(ch, i, zz, i, partner).wait_recv()
        ref, gstart, width = gcol(ch)

        def add(j):
            r = rows(j, 16)
            if ch in rs_pairs:
                at = pl.ds(pl.multiple_of(zz * 2 * br + j * 16, 16), 16)
                t = ref[at, pl.ds(gstart, width)].astype(f32) + RZP[i, r, part_of(ch)].astype(f32)
                ref[at, pl.ds(gstart, width)] = t.astype(bf16)
            else:
                t = RY[zz, r, part_of(ch)].astype(f32) + RZ[i, r, part_of(ch)].astype(f32)
                RY[zz, r, part_of(ch)] = t.astype(bf16)

        loop((2 * br if ch in rs_pairs else br) // 16, add)
        rs_z(ch, i, zz, 3, zz).start()

    def rs_pre(ch):
        if ch not in rs_pairs:
            return
        for slot in (2, 3):
            rs_z(ch, 2, z, slot, partner).wait_recv()
        ref, gstart, width = gcol(ch)

        def add(j):
            at = pl.ds(pl.multiple_of((z * 2 + 1 - y) * br + j * 16, 16), 16)
            r = pl.ds(pl.multiple_of((1 - y) * br + j * 16, 16), 16)
            t = ref[at, pl.ds(gstart, width)].astype(f32)
            t = t + RZP[2, r, part_of(ch)].astype(f32) + RZP[3, r, part_of(ch)].astype(f32)
            ref[at, pl.ds(gstart, width)] = t.astype(bf16)

        loop(br // 16, add)
        rs_y(ch, z, 1 - y).start()

    def outs(ch):
        start, width = RCH[ch]
        if start >= down0:
            pairs = [(GFD.at[pl.ds(start - down0, width), :], gdown_h.at[pl.ds(start - down0, width), :])]
        elif start >= PW:
            third = (start - PW) // (2 * FC)
            at = start - PW - 2 * FC * third
            pairs = []
            for target, low in ((ggate_h, 0), (gup_h, FC)):
                first, last = max(at, low), min(at + width, low + FC)
                if first < last:
                    held = GF.at[:, pl.ds(start - 2 * KW + first - at, last - first)]
                    pairs.append((held, target.at[:, pl.ds(third * FC + first - low, last - first)]))
        elif start == 2 * QW:
            pairs = [(GFO, gout_h)]
        elif start == 0:
            pairs = [(GF.at[:, pl.ds(0, QW)], gquery_h)]
        else:
            pairs = [
                (GF.at[:, pl.ds(QW, KW)], gkey_h),
                (GF.at[:, pl.ds(QW + KW, KW)], gvalue_h),
            ]
        return [pltpu.make_async_copy(a, b, out_sem.at[3 * ch + i]) for i, (a, b) in enumerate(pairs)]

    def rs_fin(ch):
        ref, gstart, width = gcol(ch)
        start = RCH[ch][0]
        paired = ch in rs_pairs
        rs_y(ch, z, y).wait_recv()
        if not tree:
            loop(nz - 1, lambda k: rs_z(ch, 0, z, k, z).wait_recv())
        elif not paired:
            for slot in (2, 3):
                rs_z(ch, 0, z, slot, z).wait_recv()

        def total(r0, rn, c0, cn):
            r = pl.ds(r0, rn)
            g = ref[pl.ds(pl.multiple_of(row * br + r0, 16), rn), pl.ds(gstart + c0, cn)]
            part = pl.ds(place[ch] + c0, cn)
            if paired:
                rp = pl.ds(pl.multiple_of(y * br + r0, 16), rn)
                t = RZP[2, rp, part].astype(f32) + RZP[3, rp, part].astype(f32)
                return g.astype(f32) + t + RYP[r, part].astype(f32)
            t = g.astype(f32) + RY[z, r, part].astype(f32)
            if tree:
                return t + (RZ[2, r, part].astype(f32) + RZ[3, r, part].astype(f32))
            return lax.fori_loop(0, nz - 1, lambda k, t: t + RZ[k, r, part].astype(f32), t)

        if start >= down0 or start == 2 * QW:
            for c0 in range(0, width, 128):
                t = jnp.transpose(total(0, br, c0, 128))
                if start >= down0:
                    GFD[pl.ds(start - down0 + c0, 128), :] = t
                else:
                    GFO[pl.ds(c0, 128), :] = t
        else:
            at = start - 2 * KW if start >= PW else start

            def add(i):
                r0 = pl.multiple_of(i * 16, 16)
                GF[pl.ds(r0, 16), pl.ds(at, width)] = total(r0, 16, 0, width)

            loop(br // 16, add)
        for copy in outs(ch):
            copy.start()

    def rs_done(ch):
        if ch in rs_pairs:
            rs_y(ch, z, 1 - y).wait_send()
        else:
            loop(nz, lambda zz: rs_y(ch, zz, 1 - y).wait_send())
        if tree:
            for i in range(3):
                rs_z(ch, i, zto(i), 0, partner).wait_send()
        else:
            loop(nz, lambda k: rs_z(ch, k, z, 0, z).wait_send(), 1)
        for copy in outs(ch):
            copy.wait()

    for copy in local:
        copy.start()
    bar = pltpu.get_barrier_semaphore()
    for dev in (ypeer, cpeer, xpeer, dpeer):
        pl.semaphore_signal(bar, inc=1, device_id=dev, device_id_type=MESH)

    def greet(k):
        pl.semaphore_signal(bar, inc=1, device_id=zdev((z + k) % nz), device_id_type=MESH)

    loop(nz, greet, 1)
    for i in range(4):
        local[i].wait()
    W[own, pl.ds(2 * QW, QW)] = jnp.transpose(WO[...])
    pl.semaphore_wait(bar, 4 + nz - 1)

    def load_gate_up():
        for i in range(6, 12):
            local[i].wait()

    def load_down():
        local[12].wait()
        W[own, pl.ds(down0, F)] = jnp.transpose(WD[...])

    def start_tokens():
        local[4].wait()
        tok_start()

    def start_cotangent():
        local[5].wait()
        cot_start()

    lane = lax.broadcasted_iota(jnp.int32, (1, 128), 1)
    gain_q = jnp.concatenate([gq_ref[...], gq_ref[...]], axis=1)
    gain_k = jnp.concatenate([gk_ref[...], gk_ref[...]], axis=1)
    hb = nb // 2
    spans = []
    for half in range(2):
        low = max(0, RB * half * hb - longest)
        if half * RB * hb >= longest:
            spans.append((longest + RB, RB, low, sum(s[0] for s in spans) * hb))
        else:
            spans.append((RB * hb * (half + 1), 0, 0, sum(s[0] for s in spans) * hb))

    def tables():
        VEC[...] = jnp.zeros(VEC.shape, f32)
        seg = seg_ref[...]
        first = jnp.zeros((1, T), jnp.int32)
        for d in range(ids):
            count = jnp.sum((seg == d).astype(f32), axis=1, keepdims=True).astype(jnp.int32)
            first = first + jnp.where(seg > d, count, 0)
        place = lax.broadcasted_iota(jnp.int32, (1, T), 1)
        inverse_freq = jnp.exp((lane % 32).astype(f32) * (-2.0 / 64 * math.log(rope_base)))
        CS[...] = jnp.transpose(jnp.broadcast_to((place - first).astype(f32), (128, T)))

        def fill(i):
            angle = CS[rows(i, 128), :] * inverse_freq
            sine = jnp.sin(angle)
            CS[rows(i, 128), :] = jnp.cos(angle)
            SN[rows(i, 128), :] = jnp.where(lane % 64 < 32, -sine, sine)

        loop(T // 128, fill)
        for i in range(nb):
            width, pace, start, at = spans[i // hb]
            start, at = start + pace * (i % hb), at + width * (i % hb)
            key_place = lax.broadcasted_iota(jnp.int32, (width, RB), 0) + start
            q_place, q_first = place[:, RB * i : RB * (i + 1)], first[:, RB * i : RB * (i + 1)]
            seen = (key_place <= q_place) & (key_place >= q_first)
            BIAS[pl.ds(at, width), :] = jnp.where(seen, 0.0, -1e30).astype(bf16)

    def head_mean(v):
        half_a = lax.broadcasted_iota(jnp.int32, (128, 128), 0) // 64
        half_b = lax.broadcasted_iota(jnp.int32, (128, 128), 1) // 64
        mean_matrix = jnp.where(half_a == half_b, 1.0 / 64, 0.0).astype(bf16)
        high = v.astype(bf16)
        low = (v - high.astype(f32)).astype(bf16)
        return dot_nn(high, mean_matrix) + dot_nn(low, mean_matrix)

    def turn(v):
        return jnp.where(lane % 64 < 32, pltpu.roll(v, 96, 1), pltpu.roll(v, 32, 1))

    def norm_tokens():
        tok_wait(False)
        tok_wait(True)

        def step(i):
            t = Tk[rows(i, 128), :].astype(f32)
            r = lax.rsqrt(jnp.mean(t * t, axis=1, keepdims=True) + epsilon)
            R1[rows(i, 128), :] = jnp.broadcast_to(r, (128, 128))
            Nm[rows(i, 128), :] = (t * r * ga_ref[...]).astype(bf16)

        loop(T // 128, step)

    def project():
        ag_wait(0)

        def step(i):
            r = rows(i, RB)
            PRE[r, :] = dot_nn(Nm[r, :], W[:, pl.ds(0, 2 * QW)])
            cos, sin = CS[r, :], SN[r, :]
            for p in range(3):
                v = PRE[r, pl.ds(128 * p, 128)]
                n = v * lax.rsqrt(head_mean(v * v) + epsilon)
                u = n * (gain_q if p < 2 else gain_k)
                u = (u * cos + turn(u) * sin).astype(bf16)
                if p < 2:
                    u = u * jnp.asarray(0.125, bf16)
                    QS[p, 0, r, :] = u[:, :64]
                    QS[p, 1, r, :] = u[:, 64:]
                else:
                    KS[0, r, :] = u[:, :64]
                    KS[1, r, :] = u[:, 64:]
                    ut = jnp.transpose(u)
                    KT[0, :, r] = ut[:64, :]
                    KT[1, :, r] = ut[64:, :]
            v = PRE[r, pl.ds(384, 128)].astype(bf16)
            VS[0, r, :] = v[:, :64]
            VS[1, r, :] = v[:, 64:]
            vt = jnp.transpose(v)
            VT[0, :, r] = vt[:64, :]
            VT[1, :, r] = vt[64:, :]

        loop(nb, step)

    def per_block(half, work):
        width, pace, low, at = spans[half]

        def step(n):
            i, h = n // 2, n % 2
            keys = pl.ds(pl.multiple_of(low + pace * i, RB), width) if pace else pl.ds(low, width)
            bias = BIAS[pl.ds(pl.multiple_of(at + width * i, RB), width), :].astype(f32)
            work(h, half * hb + i, keys, jnp.concatenate([bias, bias], axis=1), rows(half * hb + i, RB))

        loop(2 * hb, step)

    def attend(half):
        def work(h, i, keys, bias, r):
            q = QS[h, :, r, :].reshape(2 * RB, 64)
            e = jnp.exp(dot_nt(KS[h, keys, :], q) + bias)
            inv = 1.0 / jnp.sum(e, axis=0, keepdims=True)
            INV[h, i] = inv
            o = dot_nn(VT[h, :, keys], (e * inv).astype(bf16))
            o = jnp.concatenate([o[:, :RB], o[:, RB:]], axis=0)
            MX[r, pl.ds(pl.multiple_of(h * 128, 128), 128)] = jnp.transpose(o).astype(bf16)

        per_block(half, work)

    def attention_out(half):
        if half == 0:
            ag_wait(1)
        a_produce(half, lambda d: dot_nt(MX[rows(d, RB), :], W[:, pl.ds(2 * QW, QW)]))

    def after_attention(h):
        def use(r, at, summed):
            v = Tk[at, :].astype(f32) + summed
            RES[r, :] = v
            n = v * lax.rsqrt(jnp.mean(v * v, axis=1, keepdims=True) + epsilon)
            NF[at, :] = (n * gf_ref[...]).astype(bf16)

        a_total(h, use)
        nf_start(h)

    def ffn(j, half):
        if j == 0:
            nf_wait(half == 1)
        if half == 0:
            ag_wait(2 + j)
        elif j == 0:
            nf_done()

        def step(i):
            r = rows(own_first(half, i), RB)
            n = NF[r, :]
            gate = dot_nn(n, W[:, pl.ds(PW + 2 * FC * j, FC)])
            up = dot_nn(n, W[:, pl.ds(PW + 2 * FC * j + FC, FC)])
            sig = 1.0 / (1.0 + jnp.exp(-gate))
            act = gate * sig
            HID[r, pl.ds(FC * j, FC)] = (act * up).astype(bf16)
            GG[r, pl.ds(2 * FC * j, FC)] = (up * (sig + act * (1.0 - sig))).astype(bf16)
            GG[r, pl.ds(2 * FC * j + FC, FC)] = act.astype(bf16)

        loop(2, step)

    def grad_weights(what):
        if what < 3:
            if what == 0:
                cot_wait(False)
                cot_wait(True)
                cot_done()
            weight_grad(Ct, [(what, HID.at[:, pl.ds(FC * what, FC)])])
        elif what < 6:
            weight_grad(NF, [(what, GG.at[:, pl.ds(2 * FC * (what - 3), 2 * FC)])])
        elif what == 6:
            weight_grad(Ct, [(6, MX)])
        else:
            weight_grad(Nm, [(7, GQ.at[:, pl.ds(0, QW)]), (9, GQ.at[:, pl.ds(QW, 2 * KW)])])

    def grad_hidden(j, half):
        if half == 0:
            ag_wait(5 + j)

        def step(i):
            r = rows(other_first(half, i), RB)
            gh = dot_nn(Ct[r, :], W[:, pl.ds(down0 + FC * j, FC)])
            a, b = pl.ds(2 * FC * j, FC), pl.ds(2 * FC * j + FC, FC)
            GG[r, a] = (gh * GG[r, a].astype(f32)).astype(bf16)
            GG[r, b] = (gh * GG[r, b].astype(f32)).astype(bf16)

        loop(2, step)

    def grad_ffn_norm(half):
        if half == 0:
            a_done()
        n_produce(half, lambda d: dot_nt(GG[rows(d, RB), :], W[:, pl.ds(PW, 2 * F)]))

    def after_ffn(h):
        def use(r, at, gy):
            v = RES[r, :]
            inv = lax.rsqrt(jnp.mean(v * v, axis=1, keepdims=True) + epsilon)
            n = v * inv
            VEC[1:2, :] += jnp.sum(gy * n, axis=0, keepdims=True)
            g = gy * gf_ref[...]
            g = inv * (g - n * jnp.mean(g * n, axis=1, keepdims=True))
            Ct[at, :] = (Ct[at, :].astype(f32) + g).astype(bf16)

        n_total(h, use)
        rl_start(h)

    def grad_mixed(half):
        rl_wait(half == 1)
        if half == 0:
            DKV[...] = jnp.zeros(DKV.shape, f32)

        def step(i):
            r = rows(own_first(half, i), RB)
            g = dot_nn(Ct[r, :], W[:, pl.ds(2 * QW, QW)]).astype(bf16)
            for p in range(2):
                DO[p, 0, r, :] = g[:, 128 * p : 128 * p + 64]
                DO[p, 1, r, :] = g[:, 128 * p + 64 : 128 * p + 128]

        loop(2, step)

    def attend_back(half):
        def work(h, i, keys, bias, r):
            q = QS[h, :, r, :].reshape(2 * RB, 64)
            do = DO[h, :, r, :].reshape(2 * RB, 64)
            p = jnp.exp(dot_nt(KS[h, keys, :], q) + bias) * INV[h, i]
            dp = dot_nt(VS[h, keys, :], do)
            ds = (p * (dp - jnp.sum(p * dp, axis=0, keepdims=True))).astype(bf16)
            DKV[h, keys, :] += jnp.concatenate([dot_nn(ds, q), dot_nn(p.astype(bf16), do)], axis=1)
            g = dot_nn(KT[h, :, keys], ds) * 0.125
            g = jnp.concatenate([g[:, :RB], g[:, RB:]], axis=0)
            DQ[r, pl.ds(pl.multiple_of(h * 128, 128), 128)] = jnp.transpose(g)

        per_block(half, work)

    def project_back():
        def step(i):
            r = rows(i, RB)
            cos, sin = CS[r, :], SN[r, :]
            for p in range(3):
                if p < 2:
                    g = DQ[r, pl.ds(128 * p, 128)]
                else:
                    g = jnp.concatenate([DKV[0, r, pl.ds(0, 64)], DKV[1, r, pl.ds(0, 64)]], axis=1)
                g = g * cos - turn(g) * sin
                v = PRE[r, pl.ds(128 * p, 128)]
                inv = lax.rsqrt(head_mean(v * v) + epsilon)
                n = v * inv
                s = pl.ds(0 if p < 2 else 128, 128)
                VEC[2:3, s] += jnp.sum(g * n, axis=0, keepdims=True)
                g = g * (gain_q if p < 2 else gain_k)
                GQ[r, pl.ds(128 * p, 128)] = (inv * (g - n * head_mean(g * n))).astype(bf16)
            v = jnp.concatenate([DKV[0, r, pl.ds(64, 64)], DKV[1, r, pl.ds(64, 64)]], axis=1)
            GQ[r, pl.ds(384, 128)] = v.astype(bf16)

        loop(nb, step)

    def gn_core(i, k, xx, cc):
        return rc(
            PN.at[rows(i, RB), pl.ds(pl.multiple_of((xx * 2 + cc) * CW, CW), CW)],
            AC.at[rows(i, RB), pl.ds(pl.multiple_of(xx * CW, CW), CW)],
            gn_s.at[i, k], gn_r.at[i, k], cpeer,
        )

    def gn_x(i):
        return rc(SC.at[rows(i, RB), :], BC.at[rows(i, RB), :], gn_s.at[i, 2], gn_r.at[i, 2], xpeer)

    others = [(0, x * 2 + 1 - c, cpeer), (1, (1 - x) * 2 + c, xpeer), (2, (1 - x) * 2 + 1 - c, dpeer)]
    gains = VY.shape[0]
    vec_y = rc(VSUM.at[pl.ds(0, gains), :], VY, vec_s.at[3], vec_r.at[3], ypeer)

    def vec_copy(i, which, dev):
        return rc(VCOL.at[which], VCOL.at[which], vec_s.at[i], vec_r.at[i], dev)

    def vz_copy(k, src):
        return rc(VZ.at[src], VZ.at[src], vz_s.at[k], vz_r.at[k], zdev((z + k) % nz))

    def gn_produce():
        def step(i):
            r = rows(i, RB)
            g = dot_nt(GQ[r, :], W[:, pl.ds(0, 2 * QW)])
            PN[r, :] = g.astype(bf16)
            gn_core(i, 0, 1 - x, 1 - c).start()
            gn_core(i, 1, x, 1 - c).start()
            g = g * (Tk[r, :].astype(f32) * R1[r, pl.ds(0, 1)])
            VEC[0:1, :] += jnp.sum(g, axis=0, keepdims=True)
            s = jnp.sum(g * ga_ref[...], axis=1, keepdims=True)
            VEC[3:4, r] = jnp.transpose(jnp.broadcast_to(s, (RB, 128)))[0:1, :]

        loop(nb, step)
        for i in range(D // 128):
            s = pl.ds(128 * i, 128)
            VCOL[col, pl.ds(i, 1), :] = VEC[0:1, s]
            VCOL[col, pl.ds(D // 128 + i, 1), :] = VEC[1:2, s]
        for i in range(2):
            VCOL[col, pl.ds(D // 64 + i, 1), :] = VEC[2:3, pl.ds(128 * i, 128)]
        for i in range(T // 128):
            VCOL[col, pl.ds(gains + i, 1), :] = VEC[3:4, pl.ds(128 * i, 128)]
        for i, _, dev in others:
            vec_copy(i, col, dev).start()

    def gn_middle():
        def step(i):
            r = rows(i, RB)
            gn_core(i, 0, 1 - x, c).wait_recv()
            a = PN[r, pl.ds(pl.multiple_of(((1 - x) * 2 + c) * CW, CW), CW)].astype(f32)
            b = AC[r, pl.ds(pl.multiple_of((1 - x) * CW, CW), CW)].astype(f32)
            SC[r, :] = (a + b).astype(bf16)
            gn_x(i).start()

        loop(nb, step)

    def vec_col():
        for i, d, dev in others:
            vec_copy(i, d, dev).wait_recv()
        VSUM[...] = (VCOL[0] + VCOL[1]) + (VCOL[2] + VCOL[3])
        vec_y.start()

    def vec_row():
        vec_y.wait_recv()
        VZ[z] = VSUM[0:gains, :] + VY[...]
        loop(nz, lambda k: vz_copy(k, z).start(), 1)

    gt_copy = pltpu.make_async_copy(DQ, gt_h, out_sem.at[30])
    lo_out = pltpu.make_async_copy(LOC, lo_h, out_sem.at[31])

    def gn_finish():
        def step(i):
            r = rows(i, RB)
            gn_core(i, 1, x, c).wait_recv()
            gn_x(i).wait_recv()
            g = PN[r, mine].astype(f32) + AC[r, pl.ds(pl.multiple_of(x * CW, CW), CW)].astype(f32)
            g = (g + BC[r, :].astype(f32)) * ga_ref[:, mine]
            inv = R1[r, pl.ds(0, 1)]
            s = [VSUM[pl.ds(gains + 2 * i + j, 1), :] for j in range(2)]
            s = jnp.transpose(jnp.broadcast_to(jnp.concatenate(s, axis=1), (128, RB)))[:, 0:1] * (1.0 / D)
            n = Tk[r, mine].astype(f32) * inv
            DQ[r, :] = Ct[r, mine].astype(f32) + inv * (g - n * s)

        loop(nb, step)
        gt_copy.start()

    def lo_copy(i, d, dev):
        return rc(
            S0.at[:, pl.ds(pl.multiple_of(d * CW, CW), CW)], LOC.at[rows(col, RB), :], lo_s.at[i], lo_r.at[i], dev
        )

    def branch():
        n_done()
        for half in range(2):
            b_produce(half, lambda d: dot_nt(HID[rows(d, RB), :], W[:, pl.ds(down0, F)]))

    def block_out():
        def use(r, at, summed):
            S0[r, :] = (RES[r, :] + summed).astype(bf16)

        b_total(0, use)
        b_total(1, use)
        for i, d, dev in others:
            lo_copy(i, d, dev).start()
        LOC[rows(col, RB), :] = S0[:, mine]

    def block_out_wait():
        for i, d, dev in others:
            lo_copy(i, d, dev).wait_recv()
        lo_out.start()

    def finish():
        loop(nz, lambda k: vz_copy(k, (z + nz - k) % nz).wait_recv(), 1)
        gain_ref[...] = lax.fori_loop(1, nz, lambda k, t: t + VZ[k], VZ[0])
        tok_done()
        rl_done()
        b_done()
        for i, d, dev in others:
            lo_copy(i, d, dev).wait_send()
            vec_copy(i, col, dev).wait_send()
        vec_y.wait_send()

        def gn_done(i):
            gn_core(i, 0, 1 - x, 1 - c).wait_send()
            gn_core(i, 1, x, 1 - c).wait_send()
            gn_x(i).wait_send()

        loop(nb, gn_done)
        loop(nz, lambda k: vz_copy(k, z).wait_send(), 1)
        for ch in range(len(CH)):
            ag_done(ch)
        for ch in range(len(RCH)):
            rs_done(ch)
        gt_copy.wait()
        lo_out.wait()

    steps = {
        "gate_up": load_gate_up, "down": load_down, "toks": start_tokens, "cots": start_cotangent,
        "owny": own_y, "ownz": own_z, "fwd": forward, "tokf": tok_forward, "cotf": cot_forward,
        "tables": tables, "norm": norm_tokens, "project": project, "att": lambda half: rows_of_chip(False, half, attend), "aprod": attention_out,
        "amid": a_middle, "aft": after_attention, "nff": nf_forward, "ffn": ffn, "wg": grad_weights,
        "gh": grad_hidden, "gnfp": grad_ffn_norm, "gnfm": n_middle, "naft": after_ffn, "rlf": rl_forward,
        "gmix": grad_mixed, "ab": lambda half: rows_of_chip(True, half, attend_back), "snd": send_grad, "pb": project_back, "gnp": gn_produce, "gnm": gn_middle,
        "vc": vec_col, "vy": vec_row,
        "gnfin": gn_finish, "brp": branch, "brm": b_middle, "brf": block_out, "lof": block_out_wait,
        "mid": rs_mid, "relay": rs_relay, "pre": rs_pre, "fin": rs_fin, "end": finish,
    }
    for name, *which, who in ORDER:
        if name in ("fwd", "mid"):
            run = functools.partial(steps[name], *which, who == "m")
        else:
            run = functools.partial(steps[name], *which)
        if who == "a" or not tree:
            if who != "e" or name in ("fwd", "mid"):
                run()
        else:

            @pl.when(is_middle if who == "m" else jnp.logical_not(is_middle))
            def _():
                run()


def hand_out(*refs):
    sources, gains, targets, held, sem = refs[:9], refs[9], refs[10:19], refs[23:32], refs[32]
    loads = [pltpu.make_async_copy(a, b, sem.at[0, i]) for i, (a, b) in enumerate(zip(sources, held))]
    stores = [pltpu.make_async_copy(a, b, sem.at[1, i]) for i, (a, b) in enumerate(zip(held, targets))]
    for copy in loads:
        copy.start()
    attn, ffn, query, key = refs[19:23]
    n = attn.shape[1] // 128
    for i in range(n):
        attn[:, pl.ds(128 * i, 128)] = gains[pl.ds(i, 1), :]
        ffn[:, pl.ds(128 * i, 128)] = gains[pl.ds(n + i, 1), :]
    query[...] = gains[pl.ds(2 * n, 1), pl.ds(0, 64)] + gains[pl.ds(2 * n, 1), pl.ds(64, 64)]
    key[...] = gains[pl.ds(2 * n + 1, 1), pl.ds(0, 64)] + gains[pl.ds(2 * n + 1, 1), pl.ds(64, 64)]
    for load, store in zip(loads, stores):
        load.wait()
        store.start()
    for store in stores:
        store.wait()


def per_device(
    n_row, tokens, segment_ids, w_query, key_matrix, value_matrix, w_out, w_gate, w_up, w_down,
    norm_attn, norm_ffn, norm_query, norm_key, cotangent,
):
    T, CW = tokens.shape
    br, QW = w_query.shape
    KW = key_matrix.shape[1]
    F = w_gate.shape[1]
    D = br * n_row
    nz = n_row // 2
    PW = 2 * QW + 2 * KW
    WW = PW + 3 * F
    FC = F // 3
    nb = T // RB
    half = nb // 2 * RB
    area = (half + (longest + RB if half >= longest else 2 * half)) * (nb // 2)
    chunks = [(0, 2 * QW), (2 * QW, QW)]
    chunks += [(PW + 2 * FC * j, 2 * FC) for j in range(3)] + [(PW + 2 * F + FC * j, FC) for j in range(3)]
    start, width = chunks[4]
    last = 128
    grads = chunks[5:8] + chunks[2:4] + [(start, width - last), chunks[1], (0, QW), (start + width - last, last)]
    grads.append((QW, 2 * KW))
    gains = 2 * D // 128 + 8
    tree = nz == 4
    ag_pairs, rs_pairs = (AG_PAIRS, RS_PAIRS) if tree else ((), ())
    place, widths = [], [0, 0]
    for ch, (_, width) in enumerate(grads):
        paired = ch in rs_pairs
        place.append(widths[paired])
        widths[paired] += width
    plan = (nz, tree, chunks, grads, ag_pairs, rs_pairs, place)
    single, paired = widths[0], max(widths[1], 128)
    slots = 4 if tree else nz - 1
    vm, sem = pltpu.VMEM, pltpu.SemaphoreType.DMA
    scratch = [
        vm((D, WW), bf16), vm((QW, br), bf16), vm((F, br), bf16), vm((QW, br), f32), vm((F, br), f32),
        vm((D, 3 * F), bf16), vm((nz, br, single), bf16), vm((slots, br, single), bf16),
        vm((br, paired), bf16), vm((4, 2 * br, paired), bf16),
        vm((br, 2 * QW + 2 * F), f32), vm((T, D), bf16), vm((T, D), bf16), vm((T, D), bf16), vm((T, 128), f32),
        vm((T, 2 * QW), f32), vm((2, 2, T, 64), bf16), vm((2, T, 64), bf16), vm((2, T, 64), bf16),
        vm((2, 64, T), bf16), vm((2, 64, T), bf16), vm((2, 2, T, 64), bf16), vm((T, QW), bf16),
        vm((T, D), bf16), vm((2, RB, D), bf16), vm((RB, D), bf16), vm((RB, D), bf16), vm((RB, D), f32),
        vm((T, D), bf16), vm((T, 2 * F), bf16), vm((T, F), bf16),
        vm((T, 128), f32), vm((T, 128), f32), vm((area, RB), bf16), vm((2, nb, 1, 2 * RB), f32),
        vm((T, QW), f32), vm((2, T, 128), f32),
        vm((T, 2 * CW), bf16), vm((T, CW), bf16), vm((T, CW), bf16), vm((T, CW), bf16),
        vm((8, D), f32), vm((4, gains + T // 128, 128), f32), vm((gains + T // 128, 128), f32), vm((gains, 128), f32),
        vm((nz, gains, 128), f32),
        sem((13,)), sem((8, nz)), sem((8, nz)), sem((8, nz)), sem((8, nz)),
        sem((10, nz)), sem((10, nz)), sem((10, nz)), sem((10, nz)),
        sem((4, 2, 3)), sem((4, 2, 3)), sem((3, 4)), sem((3, 4)), sem((nb, 3)), sem((nb, 3)), sem((3,)), sem((3,)),
        sem((4,)), sem((4,)), sem((nz,)), sem((nz,)), sem((32,)),
    ]
    whole, hbm = pl.BlockSpec(memory_space=pltpu.VMEM), pl.BlockSpec(memory_space=pl.ANY)
    shape = jax.ShapeDtypeStruct
    results = (
        shape((T, CW), bf16), shape((T, CW), f32), shape((br, QW), f32), shape((br, KW), f32), shape((br, KW), f32),
        shape((QW, br), f32), shape((br, F), f32), shape((br, F), f32), shape((F, br), f32),
    )
    outs = pl.pallas_call(
        functools.partial(layer_kernel, plan),
        out_shape=results + (shape((gains, 128), f32),),
        in_specs=[hbm, whole] + [hbm] * 7 + [whole] * 4 + [hbm],
        out_specs=(hbm,) * 9 + (whole,),
        scratch_shapes=scratch,
        compiler_params=pltpu.CompilerParams(
            collective_id=0, has_side_effects=True, vmem_limit_bytes=64 * 2**20
        ),
        name="layer",
    )(
        tokens, segment_ids, w_query, key_matrix, value_matrix, w_out, w_gate, w_up, w_down,
        norm_attn[None], norm_ffn[None], norm_query[None], norm_key[None], cotangent,
    )
    gain = shape((1, D), f32)
    head_gain = shape((1, norm_query.shape[0]), f32)
    outs = pl.pallas_call(
        hand_out,
        out_shape=results + (gain, gain, head_gain, head_gain),
        in_specs=[pl.BlockSpec(memory_space=pltpu.HBM)] * 9 + [whole],
        out_specs=(pl.BlockSpec(memory_space=pltpu.HBM),) * 9 + (whole,) * 4,
        scratch_shapes=[vm(v.shape, v.dtype) for v in results] + [sem((2, 9))],
        compiler_params=pltpu.CompilerParams(vmem_limit_bytes=63 * 2**20),
        name="hand_out",
    )(*outs)
    return outs[:9] + tuple(v[0] for v in outs[9:])


def solution(mesh):
    in_specs = (
        P("row", "col"), P("row", None), P("row", "col"), P("row", "col"), P("row", "col"), P("col", "row"),
        P("row", "col"), P("row", "col"), P("col", "row"), P(), P(), P(), P(), P("row", "col"),
    )
    out_specs = (
        P("row", "col"), P("row", "col"), P("row", "col"), P("row", "col"), P("row", "col"), P("col", "row"),
        P("row", "col"), P("row", "col"), P("col", "row"), P(), P(), P(), P(),
    )
    return jax.shard_map(
        functools.partial(per_device, mesh.shape["row"]),
        mesh=mesh, in_specs=in_specs, out_specs=out_specs, check_vma=False,
    )
```

profile of v0, /device:TPU:0, one launch (start us, length us, event | category | flops | bytes accessed | tf_op | source)
XLA Modules:
  0.0 173.1 jit_solution(2143176178389432228)
XLA Ops:
  0.7 167.7 %layer.1 = (bf16[1024,256]{1,0:T(8,128)(2,1)}, f32[1024,256]{1,0:T(8,128)}, f32[128,256]{1,0:T(8,128)}, f32[128,128]{1,0:T(8,128)}, f32[128,128]{1,0:T(8,128)}, ...) custom-call(bf16[1024,256]{1,0:T(8,128)(2,1)} %tok_h.1, ...), custom_call_target="tpu_custom_call" | custom-call | tf_op jit(solution)/shard_map/layer/pallas_call | solution.py:1046
  168.4 4.5 %hand_out.1 = (bf16[1024,256]{1,0:T(8,128)(2,1)}, f32[1024,256]{1,0:T(8,128)}, f32[128,256]{1,0:T(8,128)}, f32[128,128]{1,0:T(8,128)}, f32[128,128]{1,0:T(8,128)...) custom-call(bf16[1024,256]{1,0:T(8,128)(2,1)} %get-tuple-element.36., ...), custom_call_target="tpu_custom_call" | custom-call | tf_op jit(solution)/shard_map/hand_out/pallas_call | solution.py:1062
where the time goes:
time: 173 us
  Pallas kernels  172 us (99%)
    pallas_call x1, Pallas kernels, per_device(): pl.pallas_call(functools.partial(layer_kernel, plan), out_shape=results +...  168 us
    pallas_call x1, Pallas kernels, per_device(): pl.pallas_call(hand_out, out_shape=results + (gain, gain, head_gain, head...  4.54 us

commit v1 on v0

--- a/solution.py
+++ b/solution.py
@@ -29,27 +29,28 @@
     return pl.ds(pl.multiple_of(i * n, n), n)
 
 
+LAST = 128
 AG_PAIRS, RS_PAIRS = (5, 6), (0, 1, 2)
 ORDER = [
-    ("owny", 0, "a"), ("ownz", 0, "a"), ("owny", 1, "a"), ("ownz", 1, "a"), ("gate_up", "a"), ("owny", 2, "a"),
-    ("down", "a"), ("owny", 7, "a"), ("fwd", 0, 1, "e"), ("ownz", 2, "a"), ("toks", "a"), ("tables", "a"),
-    ("cots", "a"), ("owny", 3, "a"), ("ownz", 7, "a"), ("fwd", 0, 1, "m"), ("fwd", 0, 2, "e"), ("fwd", 0, 2, "m"),
-    ("fwd", 0, 3, "e"), ("fwd", 1, 1, "e"), ("fwd", 0, 3, "m"), ("tokf", "a"), ("fwd", 1, 1, "m"),
-    ("fwd", 1, 2, "e"), ("fwd", 1, 2, "m"), ("owny", 5, "a"), ("fwd", 1, 3, "m"), ("ownz", 3, "a"), ("norm", "a"),
-    ("fwd", 1, 3, "e"), ("fwd", 2, 1, "m"), ("fwd", 2, 2, "m"), ("owny", 4, "a"), ("owny", 6, "a"),
-    ("ownz", 4, "a"), ("project", "a"), ("fwd", 2, 3, "m"), ("fwd", 3, 1, "m"), ("att", 0, "a"), ("aprod", 0, "a"),
-    ("fwd", 4, 1, "e"), ("fwd", 2, 1, "e"), ("fwd", 3, 2, "m"), ("ownz", 5, "a"), ("amid", "a"), ("fwd", 5, 1, "m"),
-    ("fwd", 3, 3, "m"), ("att", 1, "a"), ("fwd", 4, 1, "m"), ("cotf", "a"), ("fwd", 4, 2, "m"), ("fwd", 2, 2, "e"),
-    ("aprod", 1, "a"), ("fwd", 4, 3, "m"), ("fwd", 3, 1, "e"), ("fwd", 5, 2, "m"), ("fwd", 7, 1, "m"),
-    ("ownz", 6, "a"), ("aft", 0, "a"), ("fwd", 7, 1, "e"), ("fwd", 5, 3, "m"), ("fwd", 2, 3, "e"),
-    ("fwd", 7, 2, "m"), ("fwd", 7, 3, "m"), ("fwd", 5, 1, "e"), ("aft", 1, "a"), ("fwd", 3, 2, "e"),
-    ("fwd", 5, 2, "e"), ("fwd", 3, 3, "e"), ("fwd", 6, 1, "e"), ("nff", 0, "a"), ("fwd", 4, 2, "e"),
-    ("nff", 1, "a"), ("fwd", 4, 3, "e"), ("ffn", 0, 0, "a"), ("fwd", 6, 2, "e"), ("fwd", 6, 1, "m"),
-    ("fwd", 6, 2, "m"), ("fwd", 6, 3, "m"), ("ffn", 0, 1, "a"), ("wg", 0, "a"), ("ffn", 1, 0, "a"),
-    ("ffn", 1, 1, "a"), ("fwd", 5, 3, "e"), ("wg", 1, "a"), ("fwd", 7, 2, "e"), ("fwd", 6, 3, "e"),
-    ("gh", 0, 0, "a"), ("relay", 0, 0, "m"), ("gh", 0, 1, "a"), ("fwd", 7, 3, "e"), ("wg", 3, "a"),
-    ("ffn", 2, 0, "a"), ("ffn", 2, 1, "a"), ("wg", 2, "a"), ("gh", 1, 0, "a"), ("gh", 2, 0, "a"), ("gnfp", 0, "a"),
-    ("mid", 3, 0, "e"), ("gh", 1, 1, "a"), ("gnfm", "a"), ("relay", 0, 1, "m"), ("gh", 2, 1, "a"),
+    ("owny", 0, "a"), ("ownz", 0, "a"), ("out", "a"), ("owny", 1, "a"), ("ownz", 1, "a"), ("gate_up", "a"),
+    ("owny", 2, "a"), ("down", "a"), ("owny", 7, "a"), ("fwd", 0, 1, "e"), ("ownz", 2, "a"), ("toks", "a"),
+    ("tables", "a"), ("cots", "a"), ("owny", 3, "a"), ("ownz", 7, "a"), ("fwd", 0, 1, "m"), ("fwd", 0, 2, "e"),
+    ("fwd", 0, 2, "m"), ("fwd", 0, 3, "e"), ("fwd", 1, 1, "e"), ("fwd", 0, 3, "m"), ("tokf", "a"),
+    ("fwd", 1, 1, "m"), ("fwd", 1, 2, "e"), ("fwd", 1, 2, "m"), ("owny", 5, "a"), ("fwd", 1, 3, "m"),
+    ("ownz", 3, "a"), ("norm", "a"), ("fwd", 1, 3, "e"), ("fwd", 2, 1, "m"), ("fwd", 2, 2, "m"), ("owny", 4, "a"),
+    ("owny", 6, "a"), ("ownz", 4, "a"), ("project", "a"), ("fwd", 2, 3, "m"), ("fwd", 3, 1, "m"), ("att", 0, "a"),
+    ("aprod", 0, "a"), ("fwd", 4, 1, "e"), ("fwd", 2, 1, "e"), ("fwd", 3, 2, "m"), ("ownz", 5, "a"), ("amid", "a"),
+    ("fwd", 5, 1, "m"), ("fwd", 3, 3, "m"), ("att", 1, "a"), ("fwd", 4, 1, "m"), ("cotf", "a"), ("fwd", 4, 2, "m"),
+    ("fwd", 2, 2, "e"), ("aprod", 1, "a"), ("fwd", 4, 3, "m"), ("fwd", 3, 1, "e"), ("fwd", 5, 2, "m"),
+    ("fwd", 7, 1, "m"), ("ownz", 6, "a"), ("aft", 0, "a"), ("fwd", 7, 1, "e"), ("fwd", 5, 3, "m"),
+    ("fwd", 2, 3, "e"), ("fwd", 7, 2, "m"), ("fwd", 7, 3, "m"), ("fwd", 5, 1, "e"), ("aft", 1, "a"),
+    ("fwd", 3, 2, "e"), ("fwd", 5, 2, "e"), ("fwd", 3, 3, "e"), ("fwd", 6, 1, "e"), ("nff", 0, "a"),
+    ("fwd", 4, 2, "e"), ("nff", 1, "a"), ("fwd", 4, 3, "e"), ("ffn", 0, 0, "a"), ("fwd", 6, 2, "e"),
+    ("fwd", 6, 1, "m"), ("fwd", 6, 2, "m"), ("fwd", 6, 3, "m"), ("ffn", 0, 1, "a"), ("wg", 0, "a"),
+    ("ffn", 1, 0, "a"), ("ffn", 1, 1, "a"), ("fwd", 5, 3, "e"), ("wg", 1, "a"), ("fwd", 7, 2, "e"),
+    ("fwd", 6, 3, "e"), ("gh", 0, 0, "a"), ("relay", 0, 0, "m"), ("gh", 0, 1, "a"), ("fwd", 7, 3, "e"),
+    ("wg", 3, "a"), ("ffn", 2, 0, "a"), ("ffn", 2, 1, "a"), ("wg", 2, "a"), ("gh", 1, 0, "a"), ("gh", 2, 0, "a"),
+    ("gnfp", 0, "a"), ("mid", 3, 0, "e"), ("gh", 1, 1, "a"), ("gnfm", "a"), ("relay", 0, 1, "m"), ("gh", 2, 1, "a"),
     ("mid", 3, 0, "m"), ("relay", 1, 0, "m"), ("gnfp", 1, "a"), ("wg", 5, "a"), ("mid", 3, 1, "e"), ("snd", 8, "a"),
     ("naft", 0, "a"), ("wg", 4, "a"), ("mid", 5, 0, "m"), ("relay", 2, 0, "m"), ("relay", 1, 1, "m"),
     ("naft", 1, "a"), ("mid", 5, 1, "m"), ("gmix", 0, "a"), ("mid", 3, 1, "m"), ("mid", 5, 0, "e"), ("ab", 0, "a"),
@@ -73,10 +74,11 @@
 
 def layer_kernel(
     plan,
-    tok_h, seg_ref, wq_h, wk_h, wv_h, wo_h, wg_h, wu_h, wd_h, ga_ref, gf_ref, gq_ref, gk_ref, cot_h,
-    lo_h, gt_h, gquery_h, gkey_h, gvalue_h, gout_h, ggate_h, gup_h, gdown_h, gain_ref,
+    tok_h, seg_h, wq_h, wk_h, wv_h, wo_h, wg_h, wu_h, wd_h, ga_h, gf_h, gq_h, gk_h, cot_h,
+    lo_h, gt_h, gquery_h, gkey_h, gvalue_h, gout_h, ggate_h, gup_h, gdown_h, gain_h,
     W, WO, WD, GFO, GFD, G, RY, RZ, RYP, RZP, GF, Tk, Ct, Nm, R1, PRE, QS, KS, VS, KT, VT, DO, MX, PB, A0, B0, S0,
     RES, NF, GG, HID, CS, SN, BIAS, INV, DQ, DKV, AC, BC, SC, LOC, VEC, VCOL, VSUM, VY, VZ,
+    seg_ref, ga_ref, gf_ref, gq_ref, gk_ref, gain_ref,
     loc_sem, agz_s, agz_r, agy_s, agy_r, rsy_s, rsy_r, rsz_s, rsz_r,
     cag_s, cag_r, crs_s, crs_r, gn_s, gn_r, lo_s, lo_r, vec_s, vec_r, vz_s, vz_r, out_sem,
 ):
@@ -139,6 +141,7 @@
         local.append((wg_h.at[:, pl.ds(FC * j, FC)], W.at[own, pl.ds(PW + 2 * FC * j, FC)]))
         local.append((wu_h.at[:, pl.ds(FC * j, FC)], W.at[own, pl.ds(PW + 2 * FC * j + FC, FC)]))
     local.append((wd_h, WD))
+    local += [(seg_h, seg_ref), (ga_h, ga_ref), (gf_h, gf_ref), (gq_h, gq_ref), (gk_h, gk_ref)]
     local = [pltpu.make_async_copy(s, d, loc_sem.at[i]) for i, (s, d) in enumerate(local)]
 
     def wblk(ch, zz, yy):
@@ -378,7 +381,16 @@
     def send_grad(ch):
         if tree:
             for i in range(4):
-                rs_y(ch, zto(i), 1 - y).start()
+                if ch not in rs_pairs:
+                    rs_y(ch, zto(i), 1 - y).start()
+                elif i == 2:
+                    rs_z(ch, i, zto(i), i, partner).start()
+                elif i < 2:
+
+                    @pl.when(jnp.logical_not(is_middle))
+                    def _():
+                        rs_z(ch, i, zto(i), i, partner).start()
+
         else:
             loop(nz, lambda k: rs_y(ch, k, 1 - y).start())
 
@@ -526,8 +538,6 @@
         for copy in outs(ch):
             copy.wait()
 
-    for copy in local:
-        copy.start()
     bar = pltpu.get_barrier_semaphore()
     for dev in (ypeer, cpeer, xpeer, dpeer):
         pl.semaphore_signal(bar, inc=1, device_id=dev, device_id_type=MESH)
@@ -536,10 +546,15 @@
         pl.semaphore_signal(bar, inc=1, device_id=zdev((z + k) % nz), device_id_type=MESH)
 
     loop(nz, greet, 1)
-    for i in range(4):
+    for i in (0, 1, 2, 4, 13, 14, 15, 16, 17, 3, 6, 7, 8, 9, 10, 11, 5, 12):
+        local[i].start()
+    for i in range(3):
         local[i].wait()
-    W[own, pl.ds(2 * QW, QW)] = jnp.transpose(WO[...])
     pl.semaphore_wait(bar, 4 + nz - 1)
+
+    def load_out():
+        local[3].wait()
+        W[own, pl.ds(2 * QW, QW)] = jnp.transpose(WO[...])
 
     def load_gate_up():
         for i in range(6, 12):
@@ -558,8 +573,11 @@
         cot_start()
 
     lane = lax.broadcasted_iota(jnp.int32, (1, 128), 1)
-    gain_q = jnp.concatenate([gq_ref[...], gq_ref[...]], axis=1)
-    gain_k = jnp.concatenate([gk_ref[...], gk_ref[...]], axis=1)
+
+    def head_gain(p):
+        gain = (gq_ref if p < 2 else gk_ref)[...]
+        return jnp.concatenate([gain, gain], axis=1)
+
     hb = nb // 2
     spans = []
     for half in range(2):
@@ -570,6 +588,8 @@
             spans.append((RB * hb * (half + 1), 0, 0, sum(s[0] for s in spans) * hb))
 
     def tables():
+        for i in range(13, 18):
+            local[i].wait()
         VEC[...] = jnp.zeros(VEC.shape, f32)
         seg = seg_ref[...]
         first = jnp.zeros((1, T), jnp.int32)
@@ -628,7 +648,7 @@
             for p in range(3):
                 v = PRE[r, pl.ds(128 * p, 128)]
                 n = v * lax.rsqrt(head_mean(v * v) + epsilon)
-                u = n * (gain_q if p < 2 else gain_k)
+                u = n * head_gain(p)
                 u = (u * cos + turn(u) * sin).astype(bf16)
                 if p < 2:
                     u = u * jnp.asarray(0.125, bf16)
@@ -796,7 +816,7 @@
                 n = v * inv
                 s = pl.ds(0 if p < 2 else 128, 128)
                 VEC[2:3, s] += jnp.sum(g * n, axis=0, keepdims=True)
-                g = g * (gain_q if p < 2 else gain_k)
+                g = g * head_gain(p)
                 GQ[r, pl.ds(128 * p, 128)] = (inv * (g - n * head_mean(g * n))).astype(bf16)
             v = jnp.concatenate([DKV[0, r, pl.ds(64, 64)], DKV[1, r, pl.ds(64, 64)]], axis=1)
             GQ[r, pl.ds(384, 128)] = v.astype(bf16)
@@ -916,6 +936,8 @@
     def finish():
         loop(nz, lambda k: vz_copy(k, (z + nz - k) % nz).wait_recv(), 1)
         gain_ref[...] = lax.fori_loop(1, nz, lambda k, t: t + VZ[k], VZ[0])
+        gain_out = pltpu.make_async_copy(gain_ref, gain_h, out_sem.at[32])
+        gain_out.start()
         tok_done()
         rl_done()
         b_done()
@@ -937,9 +959,10 @@
             rs_done(ch)
         gt_copy.wait()
         lo_out.wait()
+        gain_out.wait()
 
     steps = {
-        "gate_up": load_gate_up, "down": load_down, "toks": start_tokens, "cots": start_cotangent,
+        "out": load_out, "gate_up": load_gate_up, "down": load_down, "toks": start_tokens, "cots": start_cotangent,
         "owny": own_y, "ownz": own_z, "fwd": forward, "tokf": tok_forward, "cotf": cot_forward,
         "tables": tables, "norm": norm_tokens, "project": project, "att": lambda half: rows_of_chip(False, half, attend), "aprod": attention_out,
         "amid": a_middle, "aft": after_attention, "nff": nf_forward, "ffn": ffn, "wg": grad_weights,
@@ -965,19 +988,22 @@
 
 
 def hand_out(*refs):
-    sources, gains, targets, held, sem = refs[:9], refs[9], refs[10:19], refs[23:32], refs[32]
+    sources, targets, held, sem = refs[:10], refs[10:23], refs[23:37], refs[37]
     loads = [pltpu.make_async_copy(a, b, sem.at[0, i]) for i, (a, b) in enumerate(zip(sources, held))]
-    stores = [pltpu.make_async_copy(a, b, sem.at[1, i]) for i, (a, b) in enumerate(zip(held, targets))]
-    for copy in loads:
+    stores = [pltpu.make_async_copy(a, b, sem.at[1, i]) for i, (a, b) in enumerate(zip(held[:9] + held[10:], targets))]
+    gains, attn, ffn, query, key = held[9:]
+    for copy in loads[9:] + loads[:9]:
         copy.start()
-    attn, ffn, query, key = refs[19:23]
+    loads[9].wait()
     n = attn.shape[1] // 128
     for i in range(n):
         attn[:, pl.ds(128 * i, 128)] = gains[pl.ds(i, 1), :]
         ffn[:, pl.ds(128 * i, 128)] = gains[pl.ds(n + i, 1), :]
     query[...] = gains[pl.ds(2 * n, 1), pl.ds(0, 64)] + gains[pl.ds(2 * n, 1), pl.ds(64, 64)]
     key[...] = gains[pl.ds(2 * n + 1, 1), pl.ds(0, 64)] + gains[pl.ds(2 * n + 1, 1), pl.ds(64, 64)]
-    for load, store in zip(loads, stores):
+    for store in stores[9:]:
+        store.start()
+    for load, store in zip(loads[:9], stores):
         load.wait()
         store.start()
     for store in stores:
@@ -1003,7 +1029,7 @@
     chunks = [(0, 2 * QW), (2 * QW, QW)]
     chunks += [(PW + 2 * FC * j, 2 * FC) for j in range(3)] + [(PW + 2 * F + FC * j, FC) for j in range(3)]
     start, width = chunks[4]
-    last = 128
+    last = LAST
     grads = chunks[5:8] + chunks[2:4] + [(start, width - last), chunks[1], (0, QW), (start + width - last, last)]
     grads.append((QW, 2 * KW))
     gains = 2 * D // 128 + 8
@@ -1031,13 +1057,14 @@
         vm((T, QW), f32), vm((2, T, 128), f32),
         vm((T, 2 * CW), bf16), vm((T, CW), bf16), vm((T, CW), bf16), vm((T, CW), bf16),
         vm((8, D), f32), vm((4, gains + T // 128, 128), f32), vm((gains + T // 128, 128), f32), vm((gains, 128), f32),
-        vm((nz, gains, 128), f32),
-        sem((13,)), sem((8, nz)), sem((8, nz)), sem((8, nz)), sem((8, nz)),
+        vm((nz, gains, 128), f32), vm((1, T), jnp.int32), vm((1, D), f32), vm((1, D), f32),
+        vm((1, norm_query.shape[0]), f32), vm((1, norm_query.shape[0]), f32), vm((gains, 128), f32),
+        sem((18,)), sem((8, nz)), sem((8, nz)), sem((8, nz)), sem((8, nz)),
         sem((10, nz)), sem((10, nz)), sem((10, nz)), sem((10, nz)),
         sem((4, 2, 3)), sem((4, 2, 3)), sem((3, 4)), sem((3, 4)), sem((nb, 3)), sem((nb, 3)), sem((3,)), sem((3,)),
-        sem((4,)), sem((4,)), sem((nz,)), sem((nz,)), sem((32,)),
+        sem((4,)), sem((4,)), sem((nz,)), sem((nz,)), sem((33,)),
     ]
-    whole, hbm = pl.BlockSpec(memory_space=pltpu.VMEM), pl.BlockSpec(memory_space=pl.ANY)
+    hbm = pl.BlockSpec(memory_space=pl.ANY)
     shape = jax.ShapeDtypeStruct
     results = (
         shape((T, CW), bf16), shape((T, CW), f32), shape((br, QW), f32), shape((br, KW), f32), shape((br, KW), f32),
@@ -1046,8 +1073,8 @@
     outs = pl.pallas_call(
         functools.partial(layer_kernel, plan),
         out_shape=results + (shape((gains, 128), f32),),
-        in_specs=[hbm, whole] + [hbm] * 7 + [whole] * 4 + [hbm],
-        out_specs=(hbm,) * 9 + (whole,),
+        in_specs=[hbm] * 14,
+        out_specs=(hbm,) * 10,
         scratch_shapes=scratch,
         compiler_params=pltpu.CompilerParams(
             collective_id=0, has_side_effects=True, vmem_limit_bytes=64 * 2**20
@@ -1062,9 +1089,10 @@
     outs = pl.pallas_call(
         hand_out,
         out_shape=results + (gain, gain, head_gain, head_gain),
-        in_specs=[pl.BlockSpec(memory_space=pltpu.HBM)] * 9 + [whole],
-        out_specs=(pl.BlockSpec(memory_space=pltpu.HBM),) * 9 + (whole,) * 4,
-        scratch_shapes=[vm(v.shape, v.dtype) for v in results] + [sem((2, 9))],
+        in_specs=[hbm] * 10,
+        out_specs=(hbm,) * 13,
+        scratch_shapes=[vm(v.shape, v.dtype) for v in results + (shape((gains, 128), f32), gain, gain, head_gain, head_gain)]
+        + [sem((2, 13))],
         compiler_params=pltpu.CompilerParams(vmem_limit_bytes=63 * 2**20),
         name="hand_out",
     )(*outs)

time: 173 us -> 171 us (0.988)
  Pallas kernels: 172 us -> 170 us
where the time goes in v1:
time: 171 us
  Pallas kernels  170 us (99%)
    pallas_call x1, Pallas kernels, per_device(): pl.pallas_call(functools.partial(layer_kernel, plan), out_shape=results +...  166 us

profile of v1, /device:TPU:0, one launch (start us, length us, event | category | flops | bytes accessed | tf_op | source)
XLA Modules:
  0.0 170.6 jit_solution(8570653554225628198)
XLA Ops:
  0.7 166.5 %layer.1 = (bf16[1024,256]{1,0:T(8,128)(2,1)}, f32[1024,256]{1,0:T(8,128)}, f32[128,256]{1,0:T(8,128)}, f32[128,128]{1,0:T(8,128)}, f32[128,128]{1,0:T(8,128)}, ...) custom-call(bf16[1024,256]{1,0:T(8,128)(2,1)} %tok_h.1, ...), custom_call_target="tpu_custom_call" | custom-call | tf_op jit(solution)/shard_map/layer/pallas_call | solution.py:1073
  167.1 3.3 %hand_out.1 = (bf16[1024,256]{1,0:T(8,128)(2,1)}, f32[1024,256]{1,0:T(8,128)}, f32[128,256]{1,0:T(8,128)}, f32[128,128]{1,0:T(8,128)}, f32[128,128]{1,0:T(8,128)...) custom-call(bf16[1024,256]{1,0:T(8,128)(2,1)} %get-tuple-element.36., ...), custom_call_target="tpu_custom_call" | custom-call | tf_op jit(solution)/shard_map/hand_out/pallas_call | solution.py:1089

commit v2 on v1

--- a/solution.py
+++ b/solution.py
@@ -30,45 +30,46 @@
 
 
 LAST = 128
-AG_PAIRS, RS_PAIRS = (5, 6), (0, 1, 2)
+AG_PAIRS, RS_PAIRS = (5, 6), (0, 1, 2, 8)
 ORDER = [
-    ("owny", 0, "a"), ("ownz", 0, "a"), ("out", "a"), ("owny", 1, "a"), ("ownz", 1, "a"), ("gate_up", "a"),
-    ("owny", 2, "a"), ("down", "a"), ("owny", 7, "a"), ("fwd", 0, 1, "e"), ("ownz", 2, "a"), ("toks", "a"),
-    ("tables", "a"), ("cots", "a"), ("owny", 3, "a"), ("ownz", 7, "a"), ("fwd", 0, 1, "m"), ("fwd", 0, 2, "e"),
-    ("fwd", 0, 2, "m"), ("fwd", 0, 3, "e"), ("fwd", 1, 1, "e"), ("fwd", 0, 3, "m"), ("tokf", "a"),
-    ("fwd", 1, 1, "m"), ("fwd", 1, 2, "e"), ("fwd", 1, 2, "m"), ("owny", 5, "a"), ("fwd", 1, 3, "m"),
-    ("ownz", 3, "a"), ("norm", "a"), ("fwd", 1, 3, "e"), ("fwd", 2, 1, "m"), ("fwd", 2, 2, "m"), ("owny", 4, "a"),
-    ("owny", 6, "a"), ("ownz", 4, "a"), ("project", "a"), ("fwd", 2, 3, "m"), ("fwd", 3, 1, "m"), ("att", 0, "a"),
-    ("aprod", 0, "a"), ("fwd", 4, 1, "e"), ("fwd", 2, 1, "e"), ("fwd", 3, 2, "m"), ("ownz", 5, "a"), ("amid", "a"),
-    ("fwd", 5, 1, "m"), ("fwd", 3, 3, "m"), ("att", 1, "a"), ("fwd", 4, 1, "m"), ("cotf", "a"), ("fwd", 4, 2, "m"),
-    ("fwd", 2, 2, "e"), ("aprod", 1, "a"), ("fwd", 4, 3, "m"), ("fwd", 3, 1, "e"), ("fwd", 5, 2, "m"),
-    ("fwd", 7, 1, "m"), ("ownz", 6, "a"), ("aft", 0, "a"), ("fwd", 7, 1, "e"), ("fwd", 5, 3, "m"),
-    ("fwd", 2, 3, "e"), ("fwd", 7, 2, "m"), ("fwd", 7, 3, "m"), ("fwd", 5, 1, "e"), ("aft", 1, "a"),
-    ("fwd", 3, 2, "e"), ("fwd", 5, 2, "e"), ("fwd", 3, 3, "e"), ("fwd", 6, 1, "e"), ("nff", 0, "a"),
-    ("fwd", 4, 2, "e"), ("nff", 1, "a"), ("fwd", 4, 3, "e"), ("ffn", 0, 0, "a"), ("fwd", 6, 2, "e"),
-    ("fwd", 6, 1, "m"), ("fwd", 6, 2, "m"), ("fwd", 6, 3, "m"), ("ffn", 0, 1, "a"), ("wg", 0, "a"),
-    ("ffn", 1, 0, "a"), ("ffn", 1, 1, "a"), ("fwd", 5, 3, "e"), ("wg", 1, "a"), ("fwd", 7, 2, "e"),
-    ("fwd", 6, 3, "e"), ("gh", 0, 0, "a"), ("relay", 0, 0, "m"), ("gh", 0, 1, "a"), ("fwd", 7, 3, "e"),
-    ("wg", 3, "a"), ("ffn", 2, 0, "a"), ("ffn", 2, 1, "a"), ("wg", 2, "a"), ("gh", 1, 0, "a"), ("gh", 2, 0, "a"),
-    ("gnfp", 0, "a"), ("mid", 3, 0, "e"), ("gh", 1, 1, "a"), ("gnfm", "a"), ("relay", 0, 1, "m"), ("gh", 2, 1, "a"),
-    ("mid", 3, 0, "m"), ("relay", 1, 0, "m"), ("gnfp", 1, "a"), ("wg", 5, "a"), ("mid", 3, 1, "e"), ("snd", 8, "a"),
-    ("naft", 0, "a"), ("wg", 4, "a"), ("mid", 5, 0, "m"), ("relay", 2, 0, "m"), ("relay", 1, 1, "m"),
-    ("naft", 1, "a"), ("mid", 5, 1, "m"), ("gmix", 0, "a"), ("mid", 3, 1, "m"), ("mid", 5, 0, "e"), ("ab", 0, "a"),
-    ("mid", 5, 2, "m"), ("mid", 3, 2, "e"), ("mid", 5, 1, "e"), ("rlf", 0, "a"), ("rlf", 1, "a"),
-    ("mid", 8, 0, "e"), ("mid", 8, 1, "e"), ("relay", 3, 0, "m"), ("relay", 2, 1, "m"), ("relay", 3, 1, "m"),
-    ("mid", 5, 2, "e"), ("mid", 8, 0, "m"), ("mid", 3, 2, "m"), ("mid", 8, 2, "e"), ("gmix", 1, "a"), ("brp", "a"),
-    ("mid", 4, 0, "e"), ("wg", 6, "a"), ("relay", 5, 0, "m"), ("brm", "a"), ("mid", 8, 1, "m"), ("mid", 4, 0, "m"),
-    ("ab", 1, "a"), ("mid", 4, 1, "e"), ("pb", "a"), ("relay", 5, 1, "m"), ("mid", 8, 2, "m"), ("mid", 4, 1, "m"),
-    ("gnp", "a"), ("mid", 6, 0, "e"), ("mid", 4, 2, "m"), ("relay", 8, 0, "m"), ("relay", 4, 0, "m"),
-    ("wg", 7, "a"), ("mid", 6, 1, "e"), ("gnm", "a"), ("mid", 6, 0, "m"), ("relay", 8, 1, "m"), ("mid", 6, 2, "e"),
-    ("brf", "a"), ("relay", 4, 1, "m"), ("mid", 6, 1, "m"), ("mid", 9, 0, "m"), ("mid", 7, 0, "e"),
-    ("mid", 7, 0, "m"), ("mid", 6, 2, "m"), ("mid", 9, 0, "e"), ("vc", "a"), ("mid", 7, 1, "e"), ("pre", 2, "e"),
-    ("pre", 1, "e"), ("relay", 6, 0, "m"), ("mid", 7, 1, "m"), ("mid", 9, 1, "m"), ("relay", 6, 1, "m"),
-    ("fin", 5, "a"), ("pre", 2, "m"), ("mid", 9, 1, "e"), ("relay", 7, 0, "m"), ("pre", 1, "m"), ("mid", 9, 2, "m"),
-    ("pre", 0, "e"), ("mid", 7, 2, "m"), ("mid", 4, 2, "e"), ("pre", 0, "m"), ("relay", 9, 0, "m"),
-    ("relay", 9, 1, "m"), ("mid", 9, 2, "e"), ("fin", 8, "a"), ("relay", 7, 1, "m"), ("fin", 6, "a"), ("vy", "a"),
-    ("fin", 4, "a"), ("mid", 7, 2, "e"), ("fin", 3, "a"), ("fin", 2, "a"), ("fin", 1, "a"), ("fin", 9, "a"),
-    ("gnfin", "a"), ("fin", 7, "a"), ("fin", 0, "a"), ("lof", "a"), ("end", "a"),
+    ("out", "a"), ("owny", 1, "a"), ("ownz", 1, "a"), ("gate_up", "a"), ("owny", 2, "a"), ("owny", 0, "a"),
+    ("toks", "a"), ("fwd", 1, 1, "e"), ("ownz", 0, "a"), ("tables", "a"), ("down", "a"), ("owny", 6, "a"),
+    ("ownz", 2, "a"), ("fwd", 0, 1, "e"), ("cots", "a"), ("fwd", 0, 1, "m"), ("fwd", 0, 2, "m"), ("fwd", 0, 3, "m"),
+    ("fwd", 0, 2, "e"), ("tokf", "a"), ("fwd", 1, 1, "m"), ("fwd", 1, 2, "m"), ("fwd", 0, 3, "e"), ("owny", 5, "a"),
+    ("fwd", 1, 3, "m"), ("fwd", 1, 2, "e"), ("ownz", 6, "a"), ("fwd", 6, 1, "e"), ("norm", "a"), ("fwd", 1, 3, "e"),
+    ("fwd", 2, 1, "m"), ("owny", 3, "a"), ("ownz", 3, "a"), ("fwd", 2, 1, "e"), ("owny", 4, "a"),
+    ("fwd", 2, 2, "m"), ("project", "a"), ("fwd", 6, 2, "e"), ("att", 0, "a"), ("fwd", 2, 3, "m"),
+    ("aprod", 0, "a"), ("owny", 7, "a"), ("amid", "a"), ("fwd", 6, 1, "m"), ("att", 1, "a"), ("ownz", 4, "a"),
+    ("fwd", 3, 1, "m"), ("fwd", 6, 3, "e"), ("aprod", 1, "a"), ("ownz", 5, "a"), ("fwd", 5, 1, "m"),
+    ("fwd", 2, 2, "e"), ("fwd", 3, 2, "m"), ("aft", 0, "a"), ("fwd", 3, 3, "m"), ("fwd", 4, 1, "m"),
+    ("fwd", 4, 2, "m"), ("fwd", 5, 1, "e"), ("ownz", 7, "a"), ("fwd", 2, 3, "e"), ("fwd", 3, 1, "e"),
+    ("aft", 1, "a"), ("fwd", 4, 3, "m"), ("fwd", 3, 2, "e"), ("fwd", 5, 2, "e"), ("cotf", "a"), ("fwd", 7, 1, "m"),
+    ("nff", 0, "a"), ("fwd", 5, 2, "m"), ("fwd", 7, 2, "m"), ("fwd", 3, 3, "e"), ("fwd", 5, 3, "e"),
+    ("fwd", 7, 3, "m"), ("fwd", 4, 1, "e"), ("ffn", 0, 0, "a"), ("nff", 1, "a"), ("ffn", 0, 1, "a"),
+    ("fwd", 5, 3, "m"), ("fwd", 6, 2, "m"), ("fwd", 6, 3, "m"), ("wg", 0, "a"), ("fwd", 4, 2, "e"),
+    ("ffn", 1, 0, "a"), ("fwd", 4, 3, "e"), ("ffn", 1, 1, "a"), ("wg", 1, "a"), ("fwd", 7, 1, "e"),
+    ("fwd", 7, 2, "e"), ("fwd", 7, 3, "e"), ("gh", 0, 0, "a"), ("gh", 0, 1, "a"), ("wg", 3, "a"),
+    ("ffn", 2, 0, "a"), ("ffn", 2, 1, "a"), ("wg", 2, "a"), ("gh", 1, 0, "a"), ("gh", 2, 0, "a"), ("gnfp", 0, "a"),
+    ("mid", 3, 0, "e"), ("relay", 0, 0, "m"), ("gnfm", "a"), ("mid", 3, 1, "e"), ("gh", 1, 1, "a"),
+    ("mid", 3, 0, "m"), ("relay", 1, 0, "m"), ("gh", 2, 1, "a"), ("relay", 2, 0, "m"), ("wg", 5, "a"),
+    ("gnfp", 1, "a"), ("naft", 0, "a"), ("wg", 4, "a"), ("mid", 3, 1, "m"), ("mid", 5, 0, "e"),
+    ("relay", 1, 1, "m"), ("mid", 0, 2, "m"), ("naft", 1, "a"), ("snd", 8, "a"), ("mid", 3, 2, "m"),
+    ("mid", 5, 0, "m"), ("gmix", 0, "a"), ("mid", 5, 1, "e"), ("relay", 0, 1, "m"), ("relay", 3, 0, "m"),
+    ("ab", 0, "a"), ("rlf", 0, "a"), ("rlf", 1, "a"), ("relay", 3, 1, "m"), ("mid", 3, 2, "e"), ("mid", 4, 0, "e"),
+    ("relay", 2, 1, "m"), ("mid", 1, 2, "m"), ("gmix", 1, "a"), ("mid", 5, 1, "m"), ("relay", 5, 0, "m"),
+    ("relay", 8, 0, "m"), ("brp", "a"), ("wg", 6, "a"), ("brm", "a"), ("mid", 4, 1, "e"), ("mid", 5, 2, "m"),
+    ("ab", 1, "a"), ("relay", 8, 1, "m"), ("pb", "a"), ("mid", 4, 2, "e"), ("relay", 5, 1, "m"), ("mid", 4, 0, "m"),
+    ("mid", 4, 1, "m"), ("gnp", "a"), ("mid", 4, 2, "m"), ("relay", 4, 0, "m"), ("relay", 4, 1, "m"),
+    ("mid", 6, 0, "e"), ("wg", 7, "a"), ("gnm", "a"), ("mid", 6, 1, "e"), ("mid", 7, 0, "e"), ("mid", 6, 0, "m"),
+    ("mid", 9, 0, "e"), ("mid", 9, 0, "m"), ("mid", 6, 2, "e"), ("relay", 6, 0, "m"), ("pre", 0, "e"),
+    ("mid", 6, 1, "m"), ("mid", 7, 1, "e"), ("pre", 2, "m"), ("mid", 7, 0, "m"), ("pre", 8, "e"),
+    ("mid", 9, 1, "e"), ("mid", 6, 2, "m"), ("mid", 9, 1, "m"), ("relay", 6, 1, "m"), ("mid", 2, 2, "m"),
+    ("vc", "a"), ("mid", 8, 2, "m"), ("mid", 5, 2, "e"), ("relay", 9, 0, "m"), ("mid", 9, 2, "m"), ("fin", 3, "a"),
+    ("mid", 7, 2, "e"), ("pre", 2, "e"), ("mid", 9, 2, "e"), ("brf", "a"), ("pre", 0, "m"), ("pre", 1, "e"),
+    ("relay", 7, 0, "m"), ("pre", 8, "m"), ("mid", 7, 1, "m"), ("mid", 7, 2, "m"), ("relay", 9, 1, "m"),
+    ("relay", 7, 1, "m"), ("vy", "a"), ("pre", 1, "m"), ("gnfin", "a"), ("fin", 0, "a"), ("fin", 4, "a"),
+    ("fin", 5, "a"), ("fin", 9, "a"), ("fin", 6, "a"), ("fin", 2, "a"), ("fin", 8, "a"), ("lof", "a"),
+    ("fin", 7, "a"), ("fin", 1, "a"), ("end", "a"),
 ]
 
 

time: 171 us -> 170 us (level)
  no operation moved by 1% of the time
where the time goes in v2:
time: 170 us
  Pallas kernels  169 us (99%)
    pallas_call x1, Pallas kernels, per_device(): pl.pallas_call(functools.partial(layer_kernel, plan), out_shape=results +...  166 us

profile of v2, /device:TPU:0, one launch (start us, length us, event | category | flops | bytes accessed | tf_op | source)
XLA Modules:
  0.0 170.2 jit_solution(4832209195306381756)
XLA Ops:
  0.7 166.0 %layer.1 = (bf16[1024,256]{1,0:T(8,128)(2,1)}, f32[1024,256]{1,0:T(8,128)}, f32[128,256]{1,0:T(8,128)}, f32[128,128]{1,0:T(8,128)}, f32[128,128]{1,0:T(8,128)}, ...) custom-call(bf16[1024,256]{1,0:T(8,128)(2,1)} %tok_h.1, ...), custom_call_target="tpu_custom_call" | custom-call | tf_op jit(solution)/shard_map/layer/pallas_call | solution.py:1074
  166.6 3.3 %hand_out.1 = (bf16[1024,256]{1,0:T(8,128)(2,1)}, f32[1024,256]{1,0:T(8,128)}, f32[128,256]{1,0:T(8,128)}, f32[128,128]{1,0:T(8,128)}, f32[128,128]{1,0:T(8,128)...) custom-call(bf16[1024,256]{1,0:T(8,128)(2,1)} %get-tuple-element.36., ...), custom_call_target="tpu_custom_call" | custom-call | tf_op jit(solution)/shard_map/hand_out/pallas_call | solution.py:1090

commit v3 on v2

--- a/solution.py
+++ b/solution.py
@@ -939,7 +939,6 @@
         gain_ref[...] = lax.fori_loop(1, nz, lambda k, t: t + VZ[k], VZ[0])
         gain_out = pltpu.make_async_copy(gain_ref, gain_h, out_sem.at[32])
         gain_out.start()
-        tok_done()
         rl_done()
         b_done()
         for i, d, dev in others:
@@ -954,20 +953,25 @@
 
         loop(nb, gn_done)
         loop(nz, lambda k: vz_copy(k, z).wait_send(), 1)
-        for ch in range(len(CH)):
-            ag_done(ch)
         for ch in range(len(RCH)):
             rs_done(ch)
         gt_copy.wait()
         lo_out.wait()
         gain_out.wait()
 
+    def gather_rest(half):
+        if half == 0:
+            tok_done()
+            for ch in range(len(CH)):
+                ag_done(ch)
+        rl_forward(half)
+
     steps = {
         "out": load_out, "gate_up": load_gate_up, "down": load_down, "toks": start_tokens, "cots": start_cotangent,
         "owny": own_y, "ownz": own_z, "fwd": forward, "tokf": tok_forward, "cotf": cot_forward,
         "tables": tables, "norm": norm_tokens, "project": project, "att": lambda half: rows_of_chip(False, half, attend), "aprod": attention_out,
         "amid": a_middle, "aft": after_attention, "nff": nf_forward, "ffn": ffn, "wg": grad_weights,
-        "gh": grad_hidden, "gnfp": grad_ffn_norm, "gnfm": n_middle, "naft": after_ffn, "rlf": rl_forward,
+        "gh": grad_hidden, "gnfp": grad_ffn_norm, "gnfm": n_middle, "naft": after_ffn, "rlf": gather_rest,
         "gmix": grad_mixed, "ab": lambda half: rows_of_chip(True, half, attend_back), "snd": send_grad, "pb": project_back, "gnp": gn_produce, "gnm": gn_middle,
         "vc": vec_col, "vy": vec_row,
         "gnfin": gn_finish, "brp": branch, "brm": b_middle, "brf": block_out, "lof": block_out_wait,

time: 170 us -> 170 us (level)
  no operation moved by 1% of the time
where the time goes in v3:
time: 170 us
  Pallas kernels  169 us (99%)
    pallas_call x1, Pallas kernels, per_device(): pl.pallas_call(functools.partial(layer_kernel, plan), out_shape=results +...  166 us

profile of v3, /device:TPU:0, one launch (start us, length us, event | category | flops | bytes accessed | tf_op | source)
XLA Modules:
  0.0 170.2 jit_solution(9184907414548939273)
XLA Ops:
  0.7 166.0 %layer.1 = (bf16[1024,256]{1,0:T(8,128)(2,1)}, f32[1024,256]{1,0:T(8,128)}, f32[128,256]{1,0:T(8,128)}, f32[128,128]{1,0:T(8,128)}, f32[128,128]{1,0:T(8,128)}, ...) custom-call(bf16[1024,256]{1,0:T(8,128)(2,1)} %tok_h.1, ...), custom_call_target="tpu_custom_call" | custom-call | tf_op jit(solution)/shard_map/layer/pallas_call | solution.py:1078
  166.6 3.3 %hand_out.1 = (bf16[1024,256]{1,0:T(8,128)(2,1)}, f32[1024,256]{1,0:T(8,128)}, f32[128,256]{1,0:T(8,128)}, f32[128,128]{1,0:T(8,128)}, f32[128,128]{1,0:T(8,128)...) custom-call(bf16[1024,256]{1,0:T(8,128)(2,1)} %get-tuple-element.36., ...), custom_call_target="tpu_custom_call" | custom-call | tf_op jit(solution)/shard_map/hand_out/pallas_call | solution.py:1094
